TPU v7x, 512 devices: a whole 4x8x8 slice. The times are simulated.
512 devices in a mesh: ctx: 128 (over z, y, core), head: 4 (over x).
Axes of the slice: x: 4, y: 8, z: 8, core: 2. Of those that a mesh axis runs over, the one named last changes fastest.
Arguments:
- queries: bfloat16 [16384, 4096], P('ctx', 'head'), may hold values from -6 to 6
- keys: bfloat16 [16384, 4096], P('ctx', 'head'), may hold values from -6 to 6
- values: bfloat16 [16384, 4096], P('ctx', 'head'), may hold values from -6 to 6
- head_gain: float32 [4096], P('head'), may hold values from 0.5 to 1.5
- w_out: bfloat16 [4096, 4096], P('head', 'ctx'), may hold values from -0.09375 to 0.09375
Outputs:
- projected: bfloat16 [16384, 4096], P('ctx', 'head')
All inputs are finite; a program needn't handle non-finite values.
Results may differ from a plain program's by a relative error of at most 0.013.
Values may be sent and summed in bfloat16 or wider, within the bound.
A program may use at most 192 MiB of HBM per device.

v0:
```python
import jax
import jax.numpy as jnp
from jax import lax
from jax.sharding import PartitionSpec as P

HD = 128


def prefix_2(value, axis, combine, identity):
    size, here = (lax.axis_size(axis), lax.axis_index(axis))
    everything = lax.all_gather(value, axis)
    start = jnp.broadcast_to(jnp.asarray(identity, value.dtype), value.shape)

    def turn(k, before):
        reached = k < here
        new = combine(before, everything[k])
        return jnp.where(reached, new, before)

    return lax.fori_loop(0, size, turn, start)


def feature(x):
    return (jax.nn.elu(x.astype(jnp.float32)) + 1.0).astype(jnp.bfloat16)


def add_states(earlier, later):
    return earlier + later


def per_device(queries, keys, values, head_gain, w_out):
    tokens = queries.shape[0]
    width = queries.shape[1]
    heads_here = width // HD
    fq = feature(queries).reshape(tokens, heads_here, HD)
    fk = feature(keys).reshape(tokens, heads_here, HD)
    vals = values.reshape(tokens, heads_here, HD)
    local = jnp.einsum("thc,thd->hcd", fk, vals, preferred_element_type=jnp.float32)
    prefix = prefix_2(local, "ctx", add_states, jnp.zeros_like(local))
    rows = lax.broadcasted_iota(jnp.int32, (1, tokens, tokens), 1)
    cols = lax.broadcasted_iota(jnp.int32, (1, tokens, tokens), 2)
    scores = jnp.einsum("thc,shc->hts", fq, fk, preferred_element_type=jnp.float32)
    weights = jnp.where(rows >= cols, scores, 0.0).astype(jnp.bfloat16)
    intra = jnp.einsum("hts,shc->thc", weights, vals, preferred_element_type=jnp.float32)
    inter = jnp.einsum(
        "thc,hcd->thd", fq.astype(jnp.float32), prefix, precision=lax.Precision.HIGHEST
    )
    mixed = intra + inter
    scale = lax.rsqrt(jnp.mean(mixed * mixed, axis=2, keepdims=True) + 1e-05)
    gain = head_gain.reshape(heads_here, HD)
    attn = (mixed * scale * gain[None]).astype(jnp.bfloat16).reshape(tokens, width)
    partial_sum = jnp.dot(
        attn, lax.all_gather(w_out, "ctx", axis=1, tiled=True), preferred_element_type=jnp.float32
    )
    summed = lax.psum_scatter(
        partial_sum.astype(jnp.bfloat16), "head", scatter_dimension=1, tiled=True
    )
    return summed


def solution(mesh):
    placed = (P("ctx", "head"), P("ctx", "head"), P("ctx", "head"), P("head"), P("head", "ctx"))
    return jax.shard_map(
        per_device, mesh=mesh, in_specs=placed, out_specs=P("ctx", "head"), check_vma=False
    )
```

profile of v0, /device:TPU:1, one launch (start us, length us, event | category | flops | bytes accessed | tf_op | source)
XLA Modules:
  0.0 441.2 jit_solution(5416678257381828798)
XLA Ops:
  6.5 1.2 fusion.7
  9.9 230.5 %all-gather.6.cloned.1.call-done = f32[1024,128,128]{2,1,0:T(8,128)} async-done(((f32[8,128,128]{2,1,0:T(8,128)}), f32[1024,128,128]{2,1,0:T(8,128)}) %all-gather.6.cloned.1.call-update) | async-done | bytes 67108880 | tf_op jit(solution)/shard_map/all_gather | solution.py:11
  240.4 160.5 %while.14 = (s32[]{:T(128)}, f32[8,128,128]{2,1,0:T(8,128)S(1)}, s32[]{:T(128)}, f32[128,8,128,128]{3,2,1,0:T(8,128)}, s32[]{:T(128)}, /*index=5*/s32[]{:T(128)}) while((s32[]{:T(128)}, f32[8,128,128]{2,1,0:T(8,128)S(1)}, s32[]{:T(128)}, f32[128,8,128,128]{3,2,1,0:T(8,128)}, s32[]{:T(128)}, /*index=5*/s32[]{:T(128)}) %tuple.33), condition=%wide.region_1.2_spmd.clone, body=%wide.region_0.1_spmd.clone.sunk | while | flops 393220 | bytes 1572957 | solution.py:19
  241.6 1.2 add_select_fusion.2
  242.9 1.2 add_select_fusion.2
  244.1 1.2 add_select_fusion.2
  245.4 1.2 add_select_fusion.2
  246.6 1.2 add_select_fusion.2
  247.9 1.2 add_select_fusion.2
  249.1 1.2 add_select_fusion.2
  250.4 1.2 add_select_fusion.2
  251.6 1.2 add_select_fusion.2
  252.9 1.2 add_select_fusion.2
  254.1 1.2 add_select_fusion.2
  255.4 1.2 add_select_fusion.2
  256.7 1.2 add_select_fusion.2
  257.9 1.2 add_select_fusion.2
  259.2 1.2 add_select_fusion.2
  260.4 1.2 add_select_fusion.2
  261.7 1.2 add_select_fusion.2
  262.9 1.2 add_select_fusion.2
  264.2 1.2 add_select_fusion.2
  265.4 1.2 add_select_fusion.2
  266.7 1.2 add_select_fusion.2
  267.9 1.2 add_select_fusion.2
  269.2 1.2 add_select_fusion.2
  270.4 1.2 add_select_fusion.2
  271.7 1.2 add_select_fusion.2
  272.9 1.2 add_select_fusion.2
  274.2 1.2 add_select_fusion.2
  275.4 1.2 add_select_fusion.2
  276.7 1.2 add_select_fusion.2
  277.9 1.2 add_select_fusion.2
  279.2 1.2 add_select_fusion.2
  280.5 1.2 add_select_fusion.2
  281.7 1.2 add_select_fusion.2
  283.0 1.2 add_select_fusion.2
  284.2 1.2 add_select_fusion.2
  285.5 1.2 add_select_fusion.2
  286.7 1.2 add_select_fusion.2
  293.0 1.2 add_select_fusion.2
  301.7 1.2 add_select_fusion.2
  303.0 1.3 add_select_fusion.2
  306.8 1.2 add_select_fusion.2
  308.0 1.2 add_select_fusion.2
  309.3 1.3 add_select_fusion.2
  310.6 1.2 add_select_fusion.2
  311.9 1.3 add_select_fusion.2
  313.2 1.3 add_select_fusion.2
  314.5 1.3 add_select_fusion.2
  315.7 1.2 add_select_fusion.2
  317.0 1.3 add_select_fusion.2
  318.3 1.2 add_select_fusion.2
  319.5 1.3 add_select_fusion.2
  320.8 1.2 add_select_fusion.2
  328.4 1.2 add_select_fusion.2
  338.4 1.2 add_select_fusion.2
  352.1 1.2 add_select_fusion.2
  362.1 1.2 add_select_fusion.2
  375.9 1.2 add_select_fusion.2
  385.9 1.2 add_select_fusion.2
  399.7 1.2 add_select_fusion.2
  402.5 7.3 %convolution_convert_fusion = bf16[128,4096]{1,0:T(8,128)(2,1)} fusion(bf16[128,1024]{0,1:T(8,128)(2,1)S(1)} %bitcast.48, bf16[1024,4096]{0,1:T(8,128)(2,1)} %all-gather.4.cloned.1.call-done), kind=kOutput, calls=%fused_computation.1 | convolution fusion | flops 1074266112 | bytes 9699328 | tf_op jit(solution)/shard_map/dot_general | solution.py:51
  409.8 24.9 %reduce-scatter.2.cloned.1.call-done = bf16[128,1024]{1,0:T(8,128)(2,1)} async-done(((bf16[128,4096]{1,0:T(8,128)(2,1)}), bf16[128,1024]{1,0:T(8,128)(2,1)}) %reduce-scatter.2.cloned.1.call-update) | async-done | bytes 262160 | tf_op jit(solution)/shard_map/reduce_scatter | solution.py:54
  (90 shorter events, 88.3 us)
Async XLA Ops:
  6.5 1.4 copy-start
  6.5 394.4 %copy-start.1 = (bf16[128,1024]{1,0:T(8,128)(2,1)S(1)}, bf16[128,1024]{1,0:T(8,128)(2,1)}, u32[]{:S(2)}) copy-start(bf16[128,1024]{1,0:T(8,128)(2,1)} %param.7) | copy-start | bytes 786436
  6.5 395.8 %copy-start.2 = (f32[1024]{0:T(1024)S(1)}, f32[1024]{0:T(1024)}, u32[]{:S(2)}) copy-start(f32[1024]{0:T(1024)} %param.10) | copy-start | bytes 12292
  6.5 233.8 %all-gather.6.cloned.1.call-start = ((), (), s32[]{:S(2)}) async-start(), calls=%async_computation.3 | async-start | bytes 67633152 | tf_op jit(solution)/shard_map/all_gather | solution.py:11
  9.0 393.5 %all-gather.4.cloned.1.call-start = ((), (), s32[]{:S(2)}) async-start(), calls=%async_computation.1 | async-start | bytes 8454144 | tf_op jit(solution)/shard_map/all_gather | solution.py:52
  9.8 424.9 %reduce-scatter.2.cloned.1.call-start = ((), (), s32[]{:S(2)}) async-start(), calls=%async_computation.2 | async-start | bytes 1310720 | tf_op jit(solution)/shard_map/reduce_scatter | solution.py:54
Sparse Core Ops, SparseCore 0:
  10.5 229.8 all-gather.5
  243.5 86.0 all-gather.3
  409.9 24.6 reduce-scatter.1
where the time goes:
time: 448 us; the launch traced here: 441 us
  waiting for transfers between devices  256 us (57%)
  other arithmetic  159 us (35%)
  between operations  13.2 us (3%)
  matrix products  9.66 us (2%)
    all_gather x1, waiting for transfers between devices, prefix_2(): everything = lax.all_gather(value, axis)  231 us
    select_n x128, other arithmetic, turn(): return jnp.where(reached, new, before)  157 us
    reduce_scatter x1, waiting for transfers between devices, per_device(): lax.psum_scatter(partial_sum.astype(jnp.bfloat16), 'head', scatter_dimens...  24.9 us
  transfers between devices with their start and end apart: 3, of which 2 were waited for; matrix products, arithmetic and copies ran while one was open for 36% of the time, Pallas kernels for 0%

commit v1 on v0

v1 whole, which is shorter than its diff:
```python
import functools

import jax
import jax.numpy as jnp
from jax import lax
from jax.experimental import pallas as pl
from jax.experimental.pallas import tpu as pltpu
from jax.sharding import PartitionSpec as P

NZ, NY, NX = 8, 8, 4
HD = 128
TOK = 128
HALF = 512
HEADS = HALF // HD
SL = 64
WB = 32
F32, BF16 = jnp.float32, jnp.bfloat16
NT = (((1,), (1,)), ((), ()))
TN = (((0,), (0,)), ((), ()))


def feature(x):
    x = x.astype(F32)
    return jnp.where(x > 0.0, x + 1.0, jnp.exp(jnp.minimum(x, 0.0))).astype(BF16)


def dot(a, b, dims=(((1,), (0,)), ((), ()))):
    return lax.dot_general(a, b, dims, preferred_element_type=F32)


def kernel(
    q_ref, k_ref, v_ref, g_ref, w_ref, o_ref,
    wa, wb, qx, kx, vx, s_out, s_in, e_buf, r_out, r_in, f_out, pf, mixed, attn,
    p2, ra, rb, p1, pm, fin, p0, sib, tot,
    s_qkv, r_qkv, s_a1, r_a1, s_b1, r_b1, s_a2, r_a2, s_b2, r_b2,
    s_p1, r_p1, s_p2, r_p2, s_p3, r_p3, s_at, r_at, s_x, r_x, s_f, r_f, s_s, r_s,
):
    me = lax.axis_index("ctx")
    x = lax.axis_index("head")
    c = lax.rem(me, 2)
    p = lax.div(me, 2)
    y = lax.rem(p, NY)
    z = lax.div(p, NY)

    def dev(zz, yy, cc, xx):
        return ((zz * NY + yy) * 2 + cc, xx)

    def up(a, d, n):
        return lax.rem(a + d, n)

    def down(a, d, n):
        return lax.rem(a + n - d, n)

    def remote(src, dst, ss, rs, to):
        return pltpu.make_async_remote_copy(
            src_ref=src, dst_ref=dst, send_sem=ss, recv_sem=rs,
            device_id=to, device_id_type=pl.DeviceIdType.MESH,
        )

    here = dev(z, y, c, x)
    sibling = dev(z, y, 1 - c, x)
    x_up, x_dn = up(x, 1, NX), down(x, 1, NX)

    barrier = pltpu.get_barrier_semaphore()

    def greet(to):
        pl.semaphore_signal(barrier, inc=1, device_id=to, device_id_type=pl.DeviceIdType.MESH)

    greet(sibling)

    @pl.loop(1, NY)
    def _(d):
        greet(dev(z, up(y, d, NY), c, x))

    @pl.loop(1, NZ)
    def _(d):
        greet(dev(up(z, d, NZ), y, c, x))

    for xx in (x_up, x_dn):
        for cc in range(2):
            greet(dev(z, y, cc, xx))

    mine = pl.ds(pl.multiple_of(c * TOK, TOK), TOK)
    other = pl.ds(pl.multiple_of((1 - c) * TOK, TOK), TOK)
    cols = pl.ds(pl.multiple_of(c * HALF, HALF), HALF)
    cols_other = pl.ds(pl.multiple_of((1 - c) * HALF, HALF), HALF)
    wa[z, y] = w_ref[:, :HALF]
    wb[z, y] = w_ref[:, HALF:]
    for src, dst in ((k_ref, kx), (v_ref, vx), (q_ref, qx)):
        dst[mine, :] = src[:, cols]

    pl.semaphore_wait(barrier, 1 + (NY - 1) + (NZ - 1) + 4)

    qkv = [
        remote(src.at[:, cols_other], dst.at[mine], s_qkv.at[i], r_qkv.at[i], sibling)
        for i, (src, dst) in enumerate(((k_ref, kx), (v_ref, vx), (q_ref, qx)))
    ]
    qkv_in = [
        remote(src.at[:, cols_other], dst.at[other], s_qkv.at[i], r_qkv.at[i], sibling)
        for i, (src, dst) in enumerate(((k_ref, kx), (v_ref, vx), (q_ref, qx)))
    ]
    for copy in qkv:
        copy.start()

    def a1(zz, yy, d, to):
        ref = wa.at[zz, yy]
        return remote(ref, ref, s_a1.at[d], r_a1.at[d], to)

    def b1(zz, yy, d, to):
        ref = wb.at[zz, yy]
        return remote(ref, ref, s_b1.at[d], r_b1.at[d], to)

    @pl.loop(1, NY)
    def _(d):
        a1(z, y, d, dev(z, up(y, d, NY), c, x)).start()

    @pl.loop(1, NZ)
    def _(d):
        b1(z, y, d, dev(up(z, d, NZ), y, c, x)).start()

    def ring(step, arriving):
        copies = []
        for way in range(2):
            gap = step if arriving else step - 1
            hop_z = dev(up(z, 1, NZ) if way == 0 else down(z, 1, NZ), y, c, x)
            hop_y = dev(z, up(y, 1, NY) if way == 0 else down(y, 1, NY), c, x)
            row = down(z, gap, NZ) if way == 0 else up(z, gap, NZ)
            col = down(y, gap, NY) if way == 0 else up(y, gap, NY)
            for j in range(2):
                if step == NY // 2 and j != way:
                    continue
                i = (way * 4 + step - 1) * 2 + j
                ref_a = wa.at[row, pl.ds(4 * j, 4)]
                ref_b = wb.at[pl.ds(4 * j, 4), col]
                copies.append(remote(ref_a, ref_a, s_a2.at[i], r_a2.at[i], hop_z))
                copies.append(remote(ref_b, ref_b, s_b2.at[i], r_b2.at[i], hop_y))
        return copies

    def ring_send(step):
        for copy in ring(step, False):
            copy.start()

    def ring_recv(step):
        for copy in ring(step, True):
            copy.wait_recv()

    qkv_in[0].wait_recv()
    qkv_in[1].wait_recv()
    fk = feature(kx[...])
    for h in range(HEADS):
        hs = slice(h * HD, (h + 1) * HD)
        state = dot(fk[:, hs], vx[:, hs], TN).astype(BF16)
        s_out[2 * h] = state[:SL]
        s_out[2 * h + 1] = state[SL:]

    def send_1(d, arriving):
        yy = down(y, d, NY) if arriving else up(y, d, NY)
        slot = s_in.at[yy if arriving else y]
        return remote(s_out.at[yy], slot, s_p1.at[d], r_p1.at[d], dev(z, yy, c, x))

    @pl.loop(1, NY)
    def _(d):
        send_1(d, False).start()

    s_in[y] = s_out[y]

    qkv_in[2].wait_recv()
    fq = feature(qx[...])
    rows = lax.broadcasted_iota(jnp.int32, (2 * TOK, 2 * TOK), 0)
    columns = lax.broadcasted_iota(jnp.int32, (2 * TOK, 2 * TOK), 1)
    for h in range(HEADS):
        hs = slice(h * HD, (h + 1) * HD)
        scores = dot(fq[:, hs], fk[:, hs], NT)
        weights = jnp.where(rows >= columns, scores, 0.0).astype(BF16)
        mixed[:, hs] = dot(weights, vx[:, hs])

    @pl.loop(1, NY)
    def _(d):
        a1(z, down(y, d, NY), d, here).wait_recv()

    @pl.loop(1, NZ)
    def _(d):
        b1(down(z, d, NZ), y, d, here).wait_recv()

    ring_send(1)

    @pl.loop(1, NY)
    def _(d):
        send_1(d, True).wait_recv()

    run = jnp.zeros((SL, HD), F32)
    for i in range(NY):
        e_buf[i] = run
        run = run + s_in[i].astype(F32)
    r_out[...] = run.astype(BF16)

    def send_2(d, arriving):
        zz = down(z, d, NZ) if arriving else up(z, d, NZ)
        slot = r_in.at[zz if arriving else z]
        return remote(r_out, slot, s_p2.at[d], r_p2.at[d], dev(zz, y, c, x))

    @pl.loop(1, NZ)
    def _(d):
        send_2(d, False).start()

    r_in[z] = r_out[...]

    ring_recv(1)
    ring_send(2)

    @pl.loop(1, NZ)
    def _(d):
        send_2(d, True).wait_recv()

    before = jnp.zeros((SL, HD), F32)
    for i in range(NZ):
        before = before + jnp.where(i < z, r_in[i].astype(F32), 0.0)
    for i in range(NY):
        f_out[i] = (before + e_buf[i]).astype(BF16)

    def send_3(d, arriving):
        yy = down(y, d, NY) if arriving else up(y, d, NY)
        slot = pf.at[yy if arriving else y]
        return remote(f_out.at[yy], slot, s_p3.at[d], r_p3.at[d], dev(z, yy, c, x))

    @pl.loop(1, NY)
    def _(d):
        send_3(d, False).start()

    pf[y] = f_out[y]

    ring_recv(2)
    ring_send(3)

    @pl.loop(1, NY)
    def _(d):
        send_3(d, True).wait_recv()

    def at_copy(h, who):
        ref = attn.at[:, pl.ds(pl.multiple_of(who * HALF + h * HD, HD), HD)]
        return remote(ref, ref, s_at.at[h], r_at.at[h], sibling)

    for h in range(HEADS):
        hs = slice(h * HD, (h + 1) * HD)
        at = pl.ds(pl.multiple_of(c * HALF + h * HD, HD), HD)
        prefix = pf[2 * h : 2 * h + 2].reshape(HD, HD)
        total = mixed[:, hs] + dot(fq[:, hs], prefix)
        scale = lax.rsqrt(jnp.mean(total * total, axis=1, keepdims=True) + 1e-05)
        attn[:, at] = (total * scale * g_ref[:, at]).astype(BF16)
        at_copy(h, c).start()

    ring_recv(3)
    ring_send(4)
    for h in range(HEADS):
        at_copy(h, 1 - c).wait_recv()
    ring_recv(4)

    def share(xx, tokens):
        w_a = wa[pl.ds(2 * xx, 2)].reshape(HALF, HALF)
        w_b = wb[pl.ds(2 * xx, 2)].reshape(HALF, HALF)
        return dot(attn[tokens, :HALF], w_a, NT) + dot(attn[tokens, HALF:], w_b, NT)

    lo, hi = pl.ds(0, TOK), pl.ds(TOK, TOK)
    x_far = up(x, 2, NX)
    far_up = remote(p2.at[0], ra, s_x.at[0], r_x.at[0], dev(z, y, c, x_up))
    far_dn = remote(p2.at[1], rb, s_x.at[1], r_x.at[1], dev(z, y, c, x_dn))
    near_up = [
        remote(p1.at[i], fin.at[c, 0], s_f.at[i], r_f.at[2 * c], dev(z, y, i, x_up)) for i in range(2)
    ]
    near_dn = [
        remote(pm.at[i], fin.at[c, 1], s_f.at[2 + i], r_f.at[2 * c + 1], dev(z, y, i, x_dn))
        for i in range(2)
    ]
    p2[0] = share(x_far, lo).astype(BF16)
    far_up.start()
    p2[1] = share(x_far, hi).astype(BF16)
    far_dn.start()
    p1[1] = share(x_up, hi).astype(BF16)
    near_up[1].start()
    pm[0] = share(x_dn, lo).astype(BF16)
    near_dn[0].start()
    part_up = share(x_up, lo)
    far_up.wait_recv()
    p1[0] = (part_up + ra[...].astype(F32)).astype(BF16)
    near_up[0].start()
    part_dn = share(x_dn, hi)
    far_dn.wait_recv()
    pm[1] = (part_dn + rb[...].astype(F32)).astype(BF16)
    near_dn[1].start()
    p0[...] = share(x, other).astype(BF16)
    across = remote(p0, sib, s_s, r_s, sibling)
    across.start()
    own = share(x, mine)

    for i in range(4):
        remote(fin.at[i // 2, i % 2], fin.at[i // 2, i % 2], s_f.at[i], r_f.at[i], here).wait_recv()
    across.wait_recv()
    tot[c] = own + fin[c, 0].astype(F32) + fin[c, 1].astype(F32)
    tot[1 - c] = sib[...].astype(F32) + fin[1 - c, 0].astype(F32) + fin[1 - c, 1].astype(F32)

    run_of = lax.div(lax.broadcasted_iota(jnp.int32, (TOK, HD), 1), WB)
    for j in range(HALF // HD):
        a = tot[0, :, j * HD : (j + 1) * HD]
        b = tot[1, :, j * HD : (j + 1) * HD]
        a_r, b_r = pltpu.roll(a, 32, 1), pltpu.roll(b, 32, 1)
        a_l, b_l = pltpu.roll(a, 96, 1), pltpu.roll(b, 96, 1)
        a_h, b_h = pltpu.roll(a, 64, 1), pltpu.roll(b, 64, 1)

        def pick(t0, t1, t2, t3):
            low = jnp.where(run_of == 0, t0, t1)
            high = jnp.where(run_of == 2, t2, t3)
            return jnp.where(run_of < 2, low, high).astype(BF16)

        o_ref[:, 2 * j * HD : (2 * j + 1) * HD] = pick(a, b_r, a_r, b_h)
        o_ref[:, (2 * j + 1) * HD : (2 * j + 2) * HD] = pick(a_h, b_l, a_l, b)

    for copy in qkv:
        copy.wait_send()

    @pl.loop(1, NY)
    def _(d):
        a1(z, y, d, here).wait_send()
        b1(z, y, d, here).wait_send()
        send_1(d, False).wait_send()
        send_2(d, False).wait_send()
        send_3(d, False).wait_send()

    for step in range(1, 5):
        for copy in ring(step, False):
            copy.wait_send()
    for h in range(HEADS):
        at_copy(h, c).wait_send()
    for copy in (far_up, far_dn, *near_up, *near_dn, across):
        copy.wait_send()


def per_device(queries, keys, values, head_gain, w_out):
    dma = pltpu.SemaphoreType.DMA
    vmem = pltpu.VMEM
    scratch = [
        vmem((NZ, NY, WB, HALF), BF16),
        vmem((NZ, NY, WB, HALF), BF16),
        vmem((2 * TOK, HALF), BF16),
        vmem((2 * TOK, HALF), BF16),
        vmem((2 * TOK, HALF), BF16),
        vmem((NY, SL, HD), BF16),
        vmem((NY, SL, HD), BF16),
        vmem((NY, SL, HD), F32),
        vmem((SL, HD), BF16),
        vmem((NZ, SL, HD), BF16),
        vmem((NY, SL, HD), BF16),
        vmem((NY, SL, HD), BF16),
        vmem((2 * TOK, HALF), F32),
        vmem((2 * TOK, 2 * HALF), BF16),
        vmem((2, TOK, HALF), BF16),
        vmem((TOK, HALF), BF16),
        vmem((TOK, HALF), BF16),
        vmem((2, TOK, HALF), BF16),
        vmem((2, TOK, HALF), BF16),
        vmem((2, 2, TOK, HALF), BF16),
        vmem((TOK, HALF), BF16),
        vmem((TOK, HALF), BF16),
        vmem((2, TOK, HALF), F32),
        dma((3,)), dma((3,)),
        dma((8,)), dma((8,)), dma((8,)), dma((8,)),
        dma((16,)), dma((16,)), dma((16,)), dma((16,)),
        dma((8,)), dma((8,)), dma((8,)), dma((8,)), dma((8,)), dma((8,)),
        dma((HEADS,)), dma((HEADS,)),
        dma((2,)), dma((2,)),
        dma((4,)), dma((4,)),
        dma(()), dma(()),
    ]
    whole = pl.BlockSpec(memory_space=pltpu.VMEM)
    return pl.pallas_call(
        kernel,
        out_shape=jax.ShapeDtypeStruct(queries.shape, BF16),
        in_specs=[whole] * 5,
        out_specs=whole,
        scratch_shapes=scratch,
        compiler_params=pltpu.CompilerParams(
            collective_id=0, has_side_effects=True, vmem_limit_bytes=40 * 2**20
        ),
        cost_estimate=pl.CostEstimate(flops=2**31, bytes_accessed=2**21, transcendentals=2**19),
    )(queries, keys, values, head_gain.reshape(1, -1), w_out.T)


def solution(mesh):
    placed = (P("ctx", "head"), P("ctx", "head"), P("ctx", "head"), P("head"), P("head", "ctx"))
    return jax.shard_map(
        per_device, mesh=mesh, in_specs=placed, out_specs=P("ctx", "head"), check_vma=False
    )
```

time: 448 us -> 70.4 us (0.16); the launches traced: 441 us -> 70.1 us
  waiting for transfers between devices: 256 us -> 0 us
  other arithmetic: 159 us -> 0 us
  Pallas kernels: 0 us -> 65.1 us
  between operations: 13.2 us -> 0.01 us
  matrix products: 9.66 us -> 0 us
  local copies, waits for them, and re-layouts: 0.18 us -> 5.08 us
    all_gather x2 -> x0, waiting for transfers between devices: 231 us -> none  [the longest x1 231 us: prefix_2(): everything = lax.all_gather(value, axis)]
    select_n x128 -> x0, other arithmetic: 157 us -> none  [turn(): return jnp.where(reached, new, before)]
    pallas_call x0 -> x1, Pallas kernels: none -> 65.1 us  [per_device(): pl.pallas_call(kernel, out_shape=jax.ShapeDtypeStruct(queries.shape, BF16...]
    reduce_scatter x1 -> x0, waiting for transfers between devices: 24.9 us -> none  [per_device(): lax.psum_scatter(partial_sum.astype(jnp.bfloat16), 'head', scatter_dimens...]
    dot_general x4 -> x0, matrix products: 9.66 us -> none  [the longest x1 7.25 us: per_device(): jnp.dot(attn, lax.all_gather(w_out, 'ctx', axis=1, tiled=True), preferred...]
    unnamed x6 -> x11, local copies, waits for them, and re-layouts: 0.01 us -> 5.08 us
  transfers between devices with their start and end apart: 3 -> 0, of which waited for: 2 -> 0; matrix products, arithmetic and copies ran while one was open for 36% -> 0% of each run, Pallas kernels for 0% -> 0%
where the time goes in v1:
time: 70.4 us; the launch traced here: 70.1 us
  Pallas kernels  65.1 us (92%)
  local copies, waits for them, and re-layouts  5.08 us (7%)
    pallas_call x1, Pallas kernels, per_device(): pl.pallas_call(kernel, out_shape=jax.ShapeDtypeStruct(queries.shape, BF16...  65.1 us
    unnamed x11, local copies, waits for them, and re-layouts  5.08 us

profile of v1, /device:TPU:1, one launch (start us, length us, event | category | flops | bytes accessed | tf_op | source)
XLA Modules:
  0.0 70.1 jit_solution(9260622718381390125)
XLA Ops:
  0.0 0.0 copy-start
  0.0 0.9 %copy-done = bf16[128,1024]{1,0:T(8,128)(2,1)S(1)} copy-done((bf16[128,1024]{1,0:T(8,128)(2,1)S(1)}, bf16[128,1024]{1,0:T(8,128)(2,1)}, u32[]{:S(2)}) %copy-start) | copy-done | bytes 262168
  1.0 0.0 copy-start.1
  1.0 0.9 %copy-done.1 = bf16[128,1024]{1,0:T(8,128)(2,1)S(1)} copy-done((bf16[128,1024]{1,0:T(8,128)(2,1)S(1)}, bf16[128,1024]{1,0:T(8,128)(2,1)}, u32[]{:S(2)}) %copy-start.1) | copy-done | bytes 262168
  1.9 0.0 copy-start.2
  1.9 0.9 %copy-done.2 = bf16[128,1024]{1,0:T(8,128)(2,1)S(1)} copy-done((bf16[128,1024]{1,0:T(8,128)(2,1)S(1)}, bf16[128,1024]{1,0:T(8,128)(2,1)}, u32[]{:S(2)}) %copy-start.2) | copy-done | bytes 262168
  2.9 0.0 copy-start.3
  2.9 0.8 %copy-done.3 = bf16[1024,32]{0,1:T(8,128)(2,1)S(1)} copy-done((bf16[1024,32]{0,1:T(8,128)(2,1)S(1)}, bf16[1024,32]{0,1:T(8,128)(2,1)}, u32[]{:S(2)}) %copy-start.3) | copy-done | bytes 65560
  3.7 0.0 copy-start.4
  3.7 0.7 copy-done.4
  4.4 65.1 %shard_map.55 = bf16[128,1024]{1,0:T(8,128)(2,1)S(1)} custom-call(bf16[128,1024]{1,0:T(8,128)(2,1)S(1)} %copy-done, bf16[128,1024]{1,0:T(8,128)(2,1)S(1)} %copy-done.1, bf16[128,1024]{1,0:T(8,128)(2,1)S(1)} %copy-done.2, f32[1,1024]{1,0:T(1,128)S(1)} %bitcast.3, bf16[32,1024]{1,0:T(8,128)(2,1)S(1)} %bitcast.2), custom_call_target="tpu_custom_call" | custom-call | flops 2147483648 | bytes 2097152 | tf_op jit(solution)/shard_map/pallas_call | solution.py:374
  69.4 0.7 %copy.7 = bf16[128,1024]{1,0:T(8,128)(2,1)} copy(bf16[128,1024]{1,0:T(8,128)(2,1)S(1)} %shard_map.55) | data formatting | bytes 524288
Async XLA Ops:
  0.0 0.9 %copy-start = (bf16[128,1024]{1,0:T(8,128)(2,1)S(1)}, bf16[128,1024]{1,0:T(8,128)(2,1)}, u32[]{:S(2)}) copy-start(bf16[128,1024]{1,0:T(8,128)(2,1)} %q_ref.1) | copy-start | bytes 786436
  1.0 0.9 %copy-start.1 = (bf16[128,1024]{1,0:T(8,128)(2,1)S(1)}, bf16[128,1024]{1,0:T(8,128)(2,1)}, u32[]{:S(2)}) copy-start(bf16[128,1024]{1,0:T(8,128)(2,1)} %k_ref.1) | copy-start | bytes 786436
  1.9 0.9 %copy-start.2 = (bf16[128,1024]{1,0:T(8,128)(2,1)S(1)}, bf16[128,1024]{1,0:T(8,128)(2,1)}, u32[]{:S(2)}) copy-start(bf16[128,1024]{1,0:T(8,128)(2,1)} %v_ref.1) | copy-start | bytes 786436
  2.9 0.8 %copy-start.3 = (bf16[1024,32]{0,1:T(8,128)(2,1)S(1)}, bf16[1024,32]{0,1:T(8,128)(2,1)}, u32[]{:S(2)}) copy-start(bf16[1024,32]{0,1:T(8,128)(2,1)} %param.9) | copy-start | bytes 196612
  3.7 0.7 copy-start.4

commit v2 on v0

v2 whole, which is shorter than its diff:
```python
import jax
import jax.numpy as jnp
from jax import lax
from jax.experimental import pallas as pl
from jax.experimental.pallas import tpu as pltpu
from jax.sharding import PartitionSpec as P

NZ, NY, NX = 8, 8, 4
HD = 128
TOK = 128
HALF = 512
HEADS = HALF // HD
SL = 64
WB = 16
GROUPS = ((0, 1), (1, 2), (3, 2), (5, 2), (7, 1))
LAST = (((0, 1, 2), (3, 4)), ((3, 4), (0, 1, 2)))
ORDER = (0, 1, -1, 2, -2, 3, -3, 4)
FAR_FIRST = (4, 3, 5, 2, 6, 1, 7)
F32, BF16 = jnp.float32, jnp.bfloat16


def slot_of(rel):
    return 2 * rel - 1 if rel > 0 else -2 * rel


def feature(x):
    x = x.astype(F32)
    return jnp.where(x > 0.0, x + 1.0, jnp.exp(jnp.minimum(x, 0.0))).astype(BF16)


def dot(a, b):
    return jnp.dot(a, b, preferred_element_type=F32)


def up(a, d, n):
    return lax.rem(a + d, n)


def down(a, d, n):
    return lax.rem(a + n - d, n)


def kernel(
    q_ref, k_ref, v_ref, g_ref, w_ref, o_ref,
    gain, wa, wb, qx, kx, vx, s_out, s_in, e_buf, r_out, r_in, f_out, pf, mixed, attn,
    near, got, fin, sib, part, out_t,
    s_in0, s_qkv, r_qkv, s_line, r_line, s_ring, r_ring,
    s_p1, r_p1, s_p2, r_p2, s_p3, r_p3, s_at, r_at, s_far, r_far, s_near, r_fin, r_sib,
):
    me = lax.axis_index("ctx")
    x = lax.axis_index("head")
    c = lax.rem(me, 2)
    p = lax.div(me, 2)
    y = lax.rem(p, NY)
    z = lax.div(p, NY)

    def dev(zz, yy, cc, xx):
        return ((zz * NY + yy) * 2 + cc, xx)

    def remote(src, dst, ss, rs, to):
        return pltpu.make_async_remote_copy(
            src_ref=src, dst_ref=dst, send_sem=ss, recv_sem=rs,
            device_id=to, device_id_type=pl.DeviceIdType.MESH,
        )

    sibling = dev(z, y, 1 - c, x)
    x_up, x_dn = up(x, 1, NX), down(x, 1, NX)

    mine = pl.ds(pl.multiple_of(c * TOK, TOK), TOK)
    other = pl.ds(pl.multiple_of((1 - c) * TOK, TOK), TOK)
    cols = pl.ds(pl.multiple_of(c * HALF, HALF), HALF)
    cols_other = pl.ds(pl.multiple_of((1 - c) * HALF, HALF), HALF)
    qkv_refs = ((k_ref, kx), (v_ref, vx), (q_ref, qx))
    inputs = [
        pltpu.make_async_copy(w_ref.at[pl.ds(0, WB)], wa.at[z, 0], s_in0.at[0]),
        pltpu.make_async_copy(w_ref.at[pl.ds(WB, WB)], wb.at[y, 0], s_in0.at[1]),
    ]
    for i, (src, dst) in enumerate(qkv_refs):
        inputs.append(pltpu.make_async_copy(src.at[:, cols], dst.at[mine], s_in0.at[2 + i]))
    inputs.append(pltpu.make_async_copy(g_ref, gain, s_in0.at[5]))
    for copy in inputs:
        copy.start()

    barrier = pltpu.get_barrier_semaphore()

    def greet(to):
        pl.semaphore_signal(barrier, inc=1, device_id=to, device_id_type=pl.DeviceIdType.MESH)

    greet(sibling)

    @pl.loop(1, NY)
    def _(d):
        greet(dev(z, up(y, d, NY), c, x))

    @pl.loop(1, NZ)
    def _(d):
        greet(dev(up(z, d, NZ), y, c, x))

    for xx in (x_up, x_dn):
        for cc in range(2):
            greet(dev(z, y, cc, xx))

    def at_y(yy):
        return dev(z, yy, c, x)

    def at_z(zz):
        return dev(zz, y, c, x)

    kinds = ((wa, y, z, at_y, at_z), (wb, z, y, at_z, at_y))

    def line(kind, way, k, arriving):
        buf, u, t, at_u, _ = kinds[kind]
        sign = 1 if way else -1
        rel = 4 if k == 4 else sign * k
        dst = buf.at[t, slot_of(rel)]
        hop = (1, 2, 1, 2)[k - 1]
        src = dst if arriving else buf.at[t, slot_of(sign * (k - hop))]
        if not arriving and k < 3:
            src = w_ref.at[pl.ds(kind * WB, WB)]
        i = (kind * 2 + way) * 4 + k - 1
        to = at_u(down(u, hop, NY) if way else up(u, hop, NY))
        return remote(src, dst, s_line.at[i], r_line.at[i], to)

    def ring(kind, way, step, group, arriving):
        buf, _, t, _, at_t = kinds[kind]
        gap = step if arriving else step - 1
        row = up(t, gap, NZ) if way else down(t, gap, NZ)
        ref = buf.at[row, pl.ds(*GROUPS[group])]
        src = ref
        if step == 1 and group == 0 and not arriving:
            ref = buf.at[row, 0]
            src = w_ref.at[pl.ds(kind * WB, WB)]
        i = ((kind * 2 + way) * 4 + step - 1) * 5 + group
        to = at_t(down(t, 1, NZ) if way else up(t, 1, NZ))
        return remote(src, ref, s_ring.at[i], r_ring.at[i], to)

    both = [(kind, way) for kind in range(2) for way in range(2)]

    def ring_send(step, group):
        for kind, way in both:
            if step < 4 or group in LAST[kind][way]:
                ring(kind, way, step, group, False).start()

    def ring_recv(step, group):
        for kind, way in both:
            if step < 4 or group in LAST[kind][way]:
                ring(kind, way, step, group, True).wait_recv()
                if step < 3 or (step == 3 and group in LAST[kind][way]):
                    ring(kind, way, step + 1, group, False).start()

    def line_send(k):
        for kind, way in both:
            if k < 4 or kind == way:
                line(kind, way, k, False).start()

    def line_recv(k):
        for kind, way in both:
            if k < 4 or kind == way:
                line(kind, way, k, True).wait_recv()

    pl.semaphore_wait(barrier, 1 + (NY - 1) + (NZ - 1) + 4)

    qkv = [
        remote(src.at[:, cols_other], dst.at[mine], s_qkv.at[i], r_qkv.at[i], sibling)
        for i, (src, dst) in enumerate(qkv_refs)
    ]
    qkv_in = [
        remote(src.at[:, cols_other], dst.at[other], s_qkv.at[i], r_qkv.at[i], sibling)
        for i, (src, dst) in enumerate(qkv_refs)
    ]
    for copy in qkv:
        copy.start()
    ring_send(1, 0)
    line_send(1)
    line_send(2)

    def send_1(d, arriving):
        yy = down(y, d, NY) if arriving else up(y, d, NY)
        slot = s_in.at[yy if arriving else y]
        return remote(s_out.at[yy], slot, s_p1.at[d], r_p1.at[d], dev(z, yy, c, x))

    def send_2(d, arriving):
        zz = down(z, d, NZ) if arriving else up(z, d, NZ)
        slot = r_in.at[zz if arriving else z]
        return remote(r_out, slot, s_p2.at[d], r_p2.at[d], dev(zz, y, c, x))

    def send_3(d, arriving):
        yy = down(y, d, NY) if arriving else up(y, d, NY)
        slot = pf.at[yy if arriving else y]
        return remote(f_out.at[yy], slot, s_p3.at[d], r_p3.at[d], dev(z, yy, c, x))

    def at_copy(h, who):
        ref = attn.at[pl.ds(pl.multiple_of(who * HALF + h * HD, HD), HD)]
        return remote(ref, ref, s_at.at[h], r_at.at[h], sibling)

    held = {}

    def states():
        for copy in inputs:
            copy.wait()
        qkv_in[0].wait_recv()
        held['fk'] = fk = feature(kx[...])
        qkv_in[1].wait_recv()
        held['v_t'] = v_t = vx[...].T
        for h in range(HEADS):
            hs = slice(h * HD, (h + 1) * HD)
            state = dot(v_t[hs], fk[:, hs]).astype(BF16)
            s_out[2 * h] = state[:SL]
            s_out[2 * h + 1] = state[SL:]

        for d in FAR_FIRST:
            send_1(d, False).start()

        s_in[y] = s_out[y]

    def inside():
        qkv_in[2].wait_recv()
        fk, v_t = held['fk'], held['v_t']
        held['fq_t'] = fq_t = feature(qx[...]).T
        keys_at = lax.broadcasted_iota(jnp.int32, (2 * TOK, 2 * TOK), 0)
        query_at = lax.broadcasted_iota(jnp.int32, (2 * TOK, 2 * TOK), 1)
        for h in range(HEADS):
            hs = slice(h * HD, (h + 1) * HD)
            scores = dot(fk[:, hs], fq_t[hs])
            weights = jnp.where(keys_at <= query_at, scores, 0.0).astype(BF16)
            mixed[hs] = dot(v_t[hs], weights)

    def row_prefix():
        for d in FAR_FIRST:
            send_1(d, True).wait_recv()

        run = jnp.zeros((SL, HD), F32)
        for i in range(NY):
            e_buf[i] = run
            run = run + s_in[i].astype(F32)
        r_out[...] = run.astype(BF16)

        for d in FAR_FIRST:

            @pl.when(z + d < NZ)
            def _():
                send_2(d, False).start()

        r_in[z] = r_out[...]

    def all_prefix():
        for d in FAR_FIRST:

            @pl.when(z >= d)
            def _():
                send_2(d, True).wait_recv()

        before = jnp.zeros((SL, HD), F32)
        for i in range(NZ):
            before = before + jnp.where(i < z, r_in[i].astype(F32), 0.0)
        for i in range(NY):
            f_out[i] = (before + e_buf[i]).astype(BF16)

        for d in FAR_FIRST:
            send_3(d, False).start()

        pf[y] = f_out[y]

    def attend():
        fq_t = held['fq_t']
        gains = []
        for h in range(HEADS):
            at = pl.ds(pl.multiple_of(c * HALF + h * HD, HD), HD)
            turned = jnp.broadcast_to(gain[:, at], (HD, HD)).T
            gains.append(jnp.concatenate([turned, turned], axis=1))

        for d in FAR_FIRST:
            send_3(d, True).wait_recv()

        for h in range(HEADS):
            hs = slice(h * HD, (h + 1) * HD)
            at = pl.ds(pl.multiple_of(c * HALF + h * HD, HD), HD)
            prefix = pf[2 * h : 2 * h + 2].reshape(HD, HD)
            total = mixed[hs] + dot(prefix, fq_t[hs])
            scale = lax.rsqrt(jnp.mean(total * total, axis=0, keepdims=True) + 1e-05)
            attn[at] = (total * scale * gains[h]).astype(BF16)
            at_copy(h, c).start()

    def unit_a(i):
        zz = up(z, jnp.where(lax.rem(i, 2) == 1, lax.div(i + 1, 2), NZ - lax.div(i, 2)), NZ)
        return zz, lax.div(zz, 2), 0, lax.rem(zz, 2), lambda: wa[zz].reshape(NY * WB, 2 * HALF)

    def unit_b(rel, grp):
        xx = up(x, rel, NX)

        def blocks():
            found = []
            for zl in range(2):
                d = up(2 * xx + zl, NZ - z, NZ)
                slot = jnp.where(d <= 4, jnp.maximum(2 * d - 1, 0), 2 * NZ - 2 * d)
                for off in ORDER[4 * grp : 4 * grp + 4]:
                    found.append(wb[up(y, off % NY, NY), slot])
            return jnp.concatenate(found, axis=0)

        return NZ + 2 * xx + grp, xx, 1, grp, blocks

    def far_copy(n, i):
        rows = pl.ds(i * SL, SL)
        to = dev(z, y, c, x_dn if i else x_up)
        return remote(near.at[n, :, rows], got.at[n, i], s_far.at[n, i], r_far.at[n, i], to)

    def near_copy(n, kind, idx, way, core):
        to = dev(z, y, core, jnp.where(way == 0, x_up, x_dn))
        return remote(
            near.at[n, core], fin.at[c, kind, idx, way], s_near.at[n, core],
            r_fin.at[((c * 2 + kind) * 2 + idx) * 2 + way], to,
        )

    def sib_copy(n, kind, idx):
        i = kind * 2 + idx
        return remote(near.at[n, 1 - c], sib.at[i], s_near.at[n, 0], r_sib.at[i], sibling)

    def far_unit(n, xx, kind, idx, blocks):
        @pl.when(up(xx, NX - x, NX) == 2)
        def _():
            total = dot(blocks(), attn[...]).astype(BF16)
            for core in range(2):
                near[n, core] = total[:, core * TOK : (core + 1) * TOK]
            for i in range(2):
                far_copy(n, i).start()

    def near_unit(n, xx, kind, idx, blocks):
        rel = up(xx, NX - x, NX)

        @pl.when(lax.rem(rel, 2) == 1)
        def _():
            total = dot(blocks(), attn[...])
            way = lax.div(rel, 2)
            rows = pl.ds(pl.multiple_of(way * SL, SL), SL)
            for core in range(2):
                part[core] = total[:, core * TOK : (core + 1) * TOK]
                near[n, core] = part[core].astype(BF16)
            far_copy_in = remote(got.at[n, way], got.at[n, way], s_far.at[n, way], r_far.at[n, way], sibling)
            far_copy_in.wait_recv()
            for core in range(2):
                near[n, core, rows] = (part[core, rows] + got[n, way, core].astype(F32)).astype(BF16)
                near_copy(n, kind, idx, way, core).start()

        @pl.when(rel == 0)
        def _():
            total = dot(blocks(), attn[...]).astype(BF16)
            for core in range(2):
                near[n, core] = total[:, core * TOK : (core + 1) * TOK]
            sib_copy(n, kind, idx).start()

    def far_units(first, last, grp):
        @pl.loop(first, last)
        def _(i):
            far_unit(*unit_a(i))

        far_unit(*unit_b(2, grp))

    def near_units(first, last, grp):
        @pl.loop(first, last)
        def _(i):
            near_unit(*unit_a(i))

        for rel in (1, 3, 0):
            near_unit(*unit_b(rel, grp))

    def line_1():
        line_recv(1)
        ring_send(1, 1)

    def line_2():
        line_recv(2)
        line_send(3)
        line_send(4)
        ring_send(1, 2)

    def line_3():
        line_recv(3)
        ring_send(1, 3)
        line_recv(4)
        ring_send(1, 4)

    def swap():
        for h in range(HEADS):
            at_copy(h, 1 - c).wait_recv()

    def early_far():
        far_units(0, 5, 0)

    def early_near():
        near_units(0, 5, 0)

    def late_far():
        far_units(5, NZ, 1)

    def late_near():
        near_units(5, NZ, 1)

    def rings(*pairs):
        for pair in pairs:
            ring_recv(*pair)

    states()
    line_1()
    line_2()
    inside()
    line_3()
    rings((1, 1), (1, 2))
    row_prefix()
    rings((1, 3), (1, 4), (1, 0), (2, 1))
    all_prefix()
    rings((2, 2), (2, 3), (2, 4), (2, 0))
    attend()
    rings((3, 1), (3, 2), (3, 3), (3, 4), (3, 0))
    swap()
    early_far()
    rings((4, 0), (4, 1), (4, 2), (4, 3), (4, 4))
    late_far()
    early_near()
    late_near()
    for i in range(16):
        ref = fin.at[i // 8, (i // 4) % 2, (i // 2) % 2, i % 2]
        remote(ref, ref, s_near.at[0, 0], r_fin.at[i], sibling).wait_recv()
    for i in range(4):
        remote(sib.at[i], sib.at[i], s_near.at[0, 0], r_sib.at[i], sibling).wait_recv()

    for s in range(2):
        for kind in range(2):
            for idx in range(2):
                n = 2 * x + idx + kind * NZ
                own = jnp.where(s == c, near[n, c].astype(F32), sib[kind * 2 + idx].astype(F32))
                total = own + fin[s, kind, idx, 0].astype(F32) + fin[s, kind, idx, 1].astype(F32)
                for i in range(NY):
                    zl, off = (idx, ORDER[i]) if kind == 0 else (i // 4, ORDER[4 * idx + i % 4])
                    out_t[zl * NY + up(y, off % NY, NY), 2 * s + kind] = total[i * WB : (i + 1) * WB]
    for j in range(NY):
        o_ref[:, j * HD : (j + 1) * HD] = out_t[2 * j : 2 * j + 2].reshape(HD, HD).T.astype(BF16)

    for copy in qkv:
        copy.wait_send()

    @pl.loop(1, NY)
    def _(d):
        send_1(d, False).wait_send()
        send_3(d, False).wait_send()

        @pl.when(z + d < NZ)
        def _():
            send_2(d, False).wait_send()

    for kind, way in both:
        for k in range(1, 5):
            if k < 4 or kind == way:
                line(kind, way, k, False).wait_send()
        for step in range(1, 5):
            for group in range(5):
                if step < 4 or group in LAST[kind][way]:
                    ring(kind, way, step, group, False).wait_send()
    for h in range(HEADS):
        at_copy(h, c).wait_send()

    def unit_left(n, xx, kind, idx, blocks):
        rel = up(xx, NX - x, NX)

        @pl.when(rel == 2)
        def _():
            for i in range(2):
                far_copy(n, i).wait_send()

        @pl.when(lax.rem(rel, 2) == 1)
        def _():
            for core in range(2):
                near_copy(n, kind, idx, lax.div(rel, 2), core).wait_send()

        @pl.when(rel == 0)
        def _():
            sib_copy(n, kind, idx).wait_send()

    @pl.loop(0, NZ)
    def _(i):
        unit_left(*unit_a(i))

    for rel in range(NX):
        for grp in range(2):
            unit_left(*unit_b(rel, grp))


def per_device(queries, keys, values, head_gain, w_out):
    dma = pltpu.SemaphoreType.DMA
    vmem = pltpu.VMEM
    rows = NY * WB
    scratch = [
        vmem((1, 2 * HALF), F32),
        vmem((NZ, NY, WB, 2 * HALF), BF16),
        vmem((NY, NZ, WB, 2 * HALF), BF16),
        vmem((2 * TOK, HALF), BF16),
        vmem((2 * TOK, HALF), BF16),
        vmem((2 * TOK, HALF), BF16),
        vmem((NY, SL, HD), BF16),
        vmem((NY, SL, HD), BF16),
        vmem((NY, SL, HD), F32),
        vmem((SL, HD), BF16),
        vmem((NZ, SL, HD), BF16),
        vmem((NY, SL, HD), BF16),
        vmem((NY, SL, HD), BF16),
        vmem((HALF, 2 * TOK), F32),
        vmem((2 * HALF, 2 * TOK), BF16),
        vmem((16, 2, rows, TOK), BF16),
        vmem((16, 2, 2, SL, TOK), BF16),
        vmem((2, 2, 2, 2, rows, TOK), BF16),
        vmem((4, rows, TOK), BF16),
        vmem((2, rows, TOK), F32),
        vmem((2 * NY, 4, WB, TOK), F32),
        dma((6,)),
        dma((3,)), dma((3,)),
        dma((16,)), dma((16,)), dma((80,)), dma((80,)),
        dma((8,)), dma((8,)), dma((8,)), dma((8,)), dma((8,)), dma((8,)),
        dma((HEADS,)), dma((HEADS,)),
        dma((16, 2)), dma((16, 2)), dma((16, 2)),
        dma((16,)), dma((4,)),
    ]
    return pl.pallas_call(
        kernel,
        out_shape=jax.ShapeDtypeStruct(queries.shape, BF16),
        in_specs=[pl.BlockSpec(memory_space=pl.ANY)] * 5,
        out_specs=pl.BlockSpec(memory_space=pltpu.VMEM),
        scratch_shapes=scratch,
        compiler_params=pltpu.CompilerParams(
            collective_id=0, has_side_effects=True, vmem_limit_bytes=60 * 2**20
        ),
        cost_estimate=pl.CostEstimate(flops=2**31, bytes_accessed=2**21, transcendentals=2**19),
    )(queries, keys, values, head_gain.reshape(1, -1), w_out.T)


def solution(mesh):
    placed = (P("ctx", "head"), P("ctx", "head"), P("ctx", "head"), P("head"), P("head", "ctx"))
    return jax.shard_map(
        per_device, mesh=mesh, in_specs=placed, out_specs=P("ctx", "head"), check_vma=False
    )
```

time: 448 us -> 62.5 us (0.14); the launches traced: 441 us -> 62.4 us
  waiting for transfers between devices: 256 us -> 0 us
  other arithmetic: 159 us -> 0 us
  Pallas kernels: 0 us -> 60.7 us
  between operations: 13.2 us -> 0.01 us
  matrix products: 9.66 us -> 0 us
    all_gather x2 -> x0, waiting for transfers between devices: 231 us -> none  [the longest x1 231 us: prefix_2(): everything = lax.all_gather(value, axis)]
    select_n x128 -> x0, other arithmetic: 157 us -> none  [turn(): return jnp.where(reached, new, before)]
    pallas_call x0 -> x1, Pallas kernels: none -> 60.7 us  [per_device(): pl.pallas_call(kernel, out_shape=jax.ShapeDtypeStruct(queries.shape, BF16...]
    reduce_scatter x1 -> x0, waiting for transfers between devices: 24.9 us -> none  [per_device(): lax.psum_scatter(partial_sum.astype(jnp.bfloat16), 'head', scatter_dimens...]
    dot_general x4 -> x0, matrix products: 9.66 us -> none  [the longest x1 7.25 us: per_device(): jnp.dot(attn, lax.all_gather(w_out, 'ctx', axis=1, tiled=True), preferred...]
  transfers between devices with their start and end apart: 3 -> 0, of which waited for: 2 -> 0; matrix products, arithmetic and copies ran while one was open for 36% -> 0% of each run, Pallas kernels for 0% -> 0%
where the time goes in v2:
time: 62.5 us; the launch traced here: 62.4 us
  Pallas kernels  60.7 us (97%)
  local copies, waits for them, and re-layouts  1.67 us (3%)
    pallas_call x1, Pallas kernels, per_device(): pl.pallas_call(kernel, out_shape=jax.ShapeDtypeStruct(queries.shape, BF16...  60.7 us
    unnamed x1, local copies, waits for them, and re-layouts  1.67 us

profile of v2, /device:TPU:1, one launch (start us, length us, event | category | flops | bytes accessed | tf_op | source)
XLA Modules:
  0.0 62.4 jit_solution(15686972184921493800)
XLA Ops:
  0.0 60.7 %shard_map.55 = bf16[128,1024]{1,0:T(8,128)(2,1)} custom-call(bf16[128,1024]{1,0:T(8,128)(2,1)} %q_ref.1, bf16[128,1024]{1,0:T(8,128)(2,1)} %k_ref.1, bf16[128,1024]{1,0:T(8,128)(2,1)} %v_ref.1, f32[1,1024]{1,0:T(1,128)} %bitcast.3, bf16[32,1024]{1,0:T(8,128)(2,1)} %bitcast.2), custom_call_target="tpu_custom_call" | custom-call | flops 2147483648 | bytes 2097152 | tf_op jit(solution)/shard_map/pallas_call | solution.py:521
  60.7 1.7 %copy.7 = bf16[128,1024]{1,0:T(8,128)(2,1)} copy(bf16[128,1024]{1,0:T(8,128)(2,1)} %shard_map.55) | data formatting | bytes 524288

commit v3 on v2

--- a/solution.py
+++ b/solution.py
@@ -213,17 +213,17 @@
 
         s_in[y] = s_out[y]
 
-    def inside():
+    def queries():
         qkv_in[2].wait_recv()
-        fk, v_t = held['fk'], held['v_t']
-        held['fq_t'] = fq_t = feature(qx[...]).T
+        held["fq_t"] = feature(qx[...]).T
+
+    def inside(h):
         keys_at = lax.broadcasted_iota(jnp.int32, (2 * TOK, 2 * TOK), 0)
         query_at = lax.broadcasted_iota(jnp.int32, (2 * TOK, 2 * TOK), 1)
-        for h in range(HEADS):
-            hs = slice(h * HD, (h + 1) * HD)
-            scores = dot(fk[:, hs], fq_t[hs])
-            weights = jnp.where(keys_at <= query_at, scores, 0.0).astype(BF16)
-            mixed[hs] = dot(v_t[hs], weights)
+        hs = slice(h * HD, (h + 1) * HD)
+        scores = dot(held["fk"][:, hs], held["fq_t"][hs])
+        weights = jnp.where(keys_at <= query_at, scores, 0.0).astype(BF16)
+        mixed[hs] = dot(held["v_t"][hs], weights)
 
     def row_prefix():
         for d in FAR_FIRST:
@@ -401,37 +401,55 @@
 
     states()
     line_1()
+    queries()
     line_2()
-    inside()
+    rings((1, 1),)
+    inside(0)
     line_3()
-    rings((1, 1), (1, 2))
+    rings((1, 2),)
+    inside(1)
     row_prefix()
-    rings((1, 3), (1, 4), (1, 0), (2, 1))
+    rings((1, 3),)
+    inside(2)
+    rings((1, 4),)
+    inside(3)
+    rings((1, 0),)
+    rings((2, 1),)
     all_prefix()
-    rings((2, 2), (2, 3), (2, 4), (2, 0))
+    rings((2, 2),)
+    rings((2, 3),)
+    rings((2, 4),)
+    rings((3, 1),)
+    rings((2, 0),)
     attend()
-    rings((3, 1), (3, 2), (3, 3), (3, 4), (3, 0))
+    rings((3, 2),)
+    rings((3, 3),)
+    rings((3, 4),)
+    rings((3, 0),)
     swap()
     early_far()
-    rings((4, 0), (4, 1), (4, 2), (4, 3), (4, 4))
+    rings((4, 1),)
+    rings((4, 2),)
+    rings((4, 0),)
+    rings((4, 3),)
+    rings((4, 4),)
     late_far()
     early_near()
     late_near()
-    for i in range(16):
-        ref = fin.at[i // 8, (i // 4) % 2, (i // 2) % 2, i % 2]
-        remote(ref, ref, s_near.at[0, 0], r_fin.at[i], sibling).wait_recv()
-    for i in range(4):
-        remote(sib.at[i], sib.at[i], s_near.at[0, 0], r_sib.at[i], sibling).wait_recv()
-
-    for s in range(2):
-        for kind in range(2):
-            for idx in range(2):
-                n = 2 * x + idx + kind * NZ
-                own = jnp.where(s == c, near[n, c].astype(F32), sib[kind * 2 + idx].astype(F32))
-                total = own + fin[s, kind, idx, 0].astype(F32) + fin[s, kind, idx, 1].astype(F32)
-                for i in range(NY):
-                    zl, off = (idx, ORDER[i]) if kind == 0 else (i // 4, ORDER[4 * idx + i % 4])
-                    out_t[zl * NY + up(y, off % NY, NY), 2 * s + kind] = total[i * WB : (i + 1) * WB]
+    for kind, idx in ((1, 0), (0, 0), (0, 1), (1, 1)):
+        n = 2 * x + idx + kind * NZ
+        away = sib.at[kind * 2 + idx]
+        remote(away, away, s_near.at[0, 0], r_sib.at[kind * 2 + idx], sibling).wait_recv()
+        for s in range(2):
+            for way in range(2):
+                ref = fin.at[s, kind, idx, way]
+                i = ((s * 2 + kind) * 2 + idx) * 2 + way
+                remote(ref, ref, s_near.at[0, 0], r_fin.at[i], sibling).wait_recv()
+            own = jnp.where(s == c, near[n, c].astype(F32), sib[kind * 2 + idx].astype(F32))
+            total = own + fin[s, kind, idx, 0].astype(F32) + fin[s, kind, idx, 1].astype(F32)
+            for i in range(NY):
+                zl, off = (idx, ORDER[i]) if kind == 0 else (i // 4, ORDER[4 * idx + i % 4])
+                out_t[zl * NY + up(y, off % NY, NY), 2 * s + kind] = total[i * WB : (i + 1) * WB]
     for j in range(NY):
         o_ref[:, j * HD : (j + 1) * HD] = out_t[2 * j : 2 * j + 2].reshape(HD, HD).T.astype(BF16)
 
@@ -518,6 +536,7 @@
         dma((16, 2)), dma((16, 2)), dma((16, 2)),
         dma((16,)), dma((4,)),
     ]
+    operands = (queries, keys, values, head_gain.reshape(1, -1), w_out.T)
     return pl.pallas_call(
         kernel,
         out_shape=jax.ShapeDtypeStruct(queries.shape, BF16),
@@ -525,10 +544,10 @@
         out_specs=pl.BlockSpec(memory_space=pltpu.VMEM),
         scratch_shapes=scratch,
         compiler_params=pltpu.CompilerParams(
-            collective_id=0, has_side_effects=True, vmem_limit_bytes=60 * 2**20
+            collective_id=0, has_side_effects=True, vmem_limit_bytes=48 * 2**20
         ),
         cost_estimate=pl.CostEstimate(flops=2**31, bytes_accessed=2**21, transcendentals=2**19),
-    )(queries, keys, values, head_gain.reshape(1, -1), w_out.T)
+    )(*[pltpu.with_memory_space_constraint(a, pltpu.HBM) for a in operands])
 
 
 def solution(mesh):

time: 62.5 us -> 60.3 us (0.965)
  Pallas kernels: 60.7 us -> 59.4 us
  local copies, waits for them, and re-layouts: 1.67 us -> 0.71 us
    pallas_call x1, Pallas kernels: 60.7 us -> 59.4 us  [per_device(): pl.pallas_call(kernel, out_shape=jax.ShapeDtypeStruct(queries.shape, BF16...]
    unnamed x1, local copies, waits for them, and re-layouts: 1.67 us -> 0.71 us
where the time goes in v3:
time: 60.3 us; the launch traced here: 60.2 us
  Pallas kernels  59.4 us (99%)
  local copies, waits for them, and re-layouts  0.71 us (1%)
    pallas_call x1, Pallas kernels, per_device(): pl.pallas_call(kernel, out_shape=jax.ShapeDtypeStruct(queries.shape, BF16...  59.4 us

profile of v3, /device:TPU:1, one launch (start us, length us, event | category | flops | bytes accessed | tf_op | source)
XLA Modules:
  0.0 60.2 jit_solution(13942164092866348048)
XLA Ops:
  0.0 59.4 %shard_map.55 = bf16[128,1024]{1,0:T(8,128)(2,1)S(1)} custom-call(bf16[128,1024]{1,0:T(8,128)(2,1)} %q_ref.1, bf16[128,1024]{1,0:T(8,128)(2,1)} %k_ref.1, bf16[128,1024]{1,0:T(8,128)(2,1)} %v_ref.1, f32[1,1024]{1,0:T(1,128)} %bitcast.3, bf16[32,1024]{1,0:T(8,128)(2,1)} %bitcast.2), custom_call_target="tpu_custom_call" | custom-call | flops 2147483648 | bytes 2097152 | tf_op jit(solution)/shard_map/pallas_call | solution.py:540
  59.5 0.7 %copy.7 = bf16[128,1024]{1,0:T(8,128)(2,1)} copy(bf16[128,1024]{1,0:T(8,128)(2,1)S(1)} %shard_map.55) | data formatting | bytes 524288

commit v4 on v3

--- a/solution.py
+++ b/solution.py
@@ -42,8 +42,8 @@
 
 def kernel(
     q_ref, k_ref, v_ref, g_ref, w_ref, o_ref,
-    gain, wa, wb, qx, kx, vx, s_out, s_in, e_buf, r_out, r_in, f_out, pf, mixed, attn,
-    near, got, fin, sib, part, out_t,
+    gain, wa, wb, qx, kx, vx, fq_t, fk_s, v_t, s_out, s_in, e_buf, r_out, r_in, f_out, pf, mixed, attn,
+    near, got, fin, sib, part, keep, out_t,
     s_in0, s_qkv, r_qkv, s_line, r_line, s_ring, r_ring,
     s_p1, r_p1, s_p2, r_p2, s_p3, r_p3, s_at, r_at, s_far, r_far, s_near, r_fin, r_sib,
 ):
@@ -141,8 +141,8 @@
             if step < 4 or group in LAST[kind][way]:
                 ring(kind, way, step, group, False).start()
 
-    def ring_recv(step, group):
-        for kind, way in both:
+    def ring_recv(step, group, kinds_now=(0, 1)):
+        for kind, way in [pair for pair in both if pair[0] in kinds_now]:
             if step < 4 or group in LAST[kind][way]:
                 ring(kind, way, step, group, True).wait_recv()
                 if step < 3 or (step == 3 and group in LAST[kind][way]):
@@ -193,18 +193,21 @@
         ref = attn.at[pl.ds(pl.multiple_of(who * HALF + h * HD, HD), HD)]
         return remote(ref, ref, s_at.at[h], r_at.at[h], sibling)
 
-    held = {}
+    def turn(tokens):
+        fk_s[tokens] = feature(kx[tokens])
+        v_t[:, tokens] = vx[tokens].T
 
     def states():
         for copy in inputs:
             copy.wait()
+        turn(mine)
+        fq_t[:, mine] = feature(qx[mine]).T
         qkv_in[0].wait_recv()
-        held['fk'] = fk = feature(kx[...])
         qkv_in[1].wait_recv()
-        held['v_t'] = v_t = vx[...].T
+        turn(other)
         for h in range(HEADS):
             hs = slice(h * HD, (h + 1) * HD)
-            state = dot(v_t[hs], fk[:, hs]).astype(BF16)
+            state = dot(v_t[hs], fk_s[:, hs]).astype(BF16)
             s_out[2 * h] = state[:SL]
             s_out[2 * h + 1] = state[SL:]
 
@@ -215,15 +218,15 @@
 
     def queries():
         qkv_in[2].wait_recv()
-        held["fq_t"] = feature(qx[...]).T
+        fq_t[:, other] = feature(qx[other]).T
 
     def inside(h):
         keys_at = lax.broadcasted_iota(jnp.int32, (2 * TOK, 2 * TOK), 0)
         query_at = lax.broadcasted_iota(jnp.int32, (2 * TOK, 2 * TOK), 1)
         hs = slice(h * HD, (h + 1) * HD)
-        scores = dot(held["fk"][:, hs], held["fq_t"][hs])
+        scores = dot(fk_s[:, hs], fq_t[hs])
         weights = jnp.where(keys_at <= query_at, scores, 0.0).astype(BF16)
-        mixed[hs] = dot(held["v_t"][hs], weights)
+        mixed[hs] = dot(v_t[hs], weights)
 
     def row_prefix():
         for d in FAR_FIRST:
@@ -262,7 +265,6 @@
         pf[y] = f_out[y]
 
     def attend():
-        fq_t = held['fq_t']
         gains = []
         for h in range(HEADS):
             at = pl.ds(pl.multiple_of(c * HALF + h * HD, HD), HD)
@@ -304,16 +306,20 @@
         to = dev(z, y, c, x_dn if i else x_up)
         return remote(near.at[n, :, rows], got.at[n, i], s_far.at[n, i], r_far.at[n, i], to)
 
-    def near_copy(n, kind, idx, way, core):
+    def rows_of(half):
+        return pl.ds(pl.multiple_of(half * SL, SL), SL)
+
+    def near_copy(n, kind, idx, way, core, half):
         to = dev(z, y, core, jnp.where(way == 0, x_up, x_dn))
+        rows = rows_of(half)
         return remote(
-            near.at[n, core], fin.at[c, kind, idx, way], s_near.at[n, core],
-            r_fin.at[((c * 2 + kind) * 2 + idx) * 2 + way], to,
+            near.at[n, core, rows], fin.at[c, kind, idx, way, rows], s_near.at[n, core, half],
+            r_fin.at[((c * 2 + kind) * 2 + idx) * 2 + way, half], to,
         )
 
     def sib_copy(n, kind, idx):
         i = kind * 2 + idx
-        return remote(near.at[n, 1 - c], sib.at[i], s_near.at[n, 0], r_sib.at[i], sibling)
+        return remote(near.at[n, 1 - c], sib.at[i], s_near.at[n, 0, 0], r_sib.at[i], sibling)
 
     def far_unit(n, xx, kind, idx, blocks):
         @pl.when(up(xx, NX - x, NX) == 2)
@@ -331,15 +337,11 @@
         def _():
             total = dot(blocks(), attn[...])
             way = lax.div(rel, 2)
-            rows = pl.ds(pl.multiple_of(way * SL, SL), SL)
             for core in range(2):
                 part[core] = total[:, core * TOK : (core + 1) * TOK]
                 near[n, core] = part[core].astype(BF16)
-            far_copy_in = remote(got.at[n, way], got.at[n, way], s_far.at[n, way], r_far.at[n, way], sibling)
-            far_copy_in.wait_recv()
-            for core in range(2):
-                near[n, core, rows] = (part[core, rows] + got[n, way, core].astype(F32)).astype(BF16)
-                near_copy(n, kind, idx, way, core).start()
+                keep[n, core] = part[core, rows_of(way)]
+                near_copy(n, kind, idx, way, core, 1 - way).start()
 
         @pl.when(rel == 0)
         def _():
@@ -348,6 +350,18 @@
                 near[n, core] = total[:, core * TOK : (core + 1) * TOK]
             sib_copy(n, kind, idx).start()
 
+    def sum_unit(n, xx, kind, idx, blocks):
+        rel = up(xx, NX - x, NX)
+
+        @pl.when(lax.rem(rel, 2) == 1)
+        def _():
+            way = lax.div(rel, 2)
+            ref = got.at[n, way]
+            remote(ref, ref, s_far.at[n, way], r_far.at[n, way], sibling).wait_recv()
+            for core in range(2):
+                near[n, core, rows_of(way)] = (keep[n, core] + got[n, way, core].astype(F32)).astype(BF16)
+                near_copy(n, kind, idx, way, core, way).start()
+
     def far_units(first, last, grp):
         @pl.loop(first, last)
         def _(i):
@@ -362,6 +376,14 @@
 
         for rel in (1, 3, 0):
             near_unit(*unit_b(rel, grp))
+
+    def sum_units(first, last, grp):
+        @pl.loop(first, last)
+        def _(i):
+            sum_unit(*unit_a(i))
+
+        for rel in (1, 3):
+            sum_unit(*unit_b(rel, grp))
 
     def line_1():
         line_recv(1)
@@ -395,6 +417,12 @@
     def late_near():
         near_units(5, NZ, 1)
 
+    def early_sum():
+        sum_units(0, 5, 0)
+
+    def late_sum():
+        sum_units(5, NZ, 1)
+
     def rings(*pairs):
         for pair in pairs:
             ring_recv(*pair)
@@ -403,48 +431,51 @@
     line_1()
     queries()
     line_2()
-    rings((1, 1),)
+    ring_recv(1, 1)
     inside(0)
     line_3()
-    rings((1, 2),)
+    ring_recv(1, 2)
     inside(1)
     row_prefix()
-    rings((1, 3),)
+    ring_recv(1, 3)
     inside(2)
-    rings((1, 4),)
+    ring_recv(1, 4)
     inside(3)
-    rings((1, 0),)
-    rings((2, 1),)
+    ring_recv(1, 0)
+    ring_recv(2, 1)
     all_prefix()
-    rings((2, 2),)
-    rings((2, 3),)
-    rings((2, 4),)
-    rings((3, 1),)
-    rings((2, 0),)
+    ring_recv(2, 2)
+    ring_recv(2, 3)
+    ring_recv(2, 4)
+    ring_recv(3, 1)
+    ring_recv(2, 0)
     attend()
-    rings((3, 2),)
-    rings((3, 3),)
-    rings((3, 4),)
-    rings((3, 0),)
+    ring_recv(3, 2)
+    ring_recv(3, 3)
+    ring_recv(3, 4)
+    ring_recv(3, 0)
     swap()
     early_far()
-    rings((4, 1),)
-    rings((4, 2),)
-    rings((4, 0),)
-    rings((4, 3),)
-    rings((4, 4),)
+    ring_recv(4, 1)
+    ring_recv(4, 2)
+    ring_recv(4, 0)
+    ring_recv(4, 3)
+    ring_recv(4, 4)
     late_far()
     early_near()
     late_near()
+    early_sum()
+    late_sum()
     for kind, idx in ((1, 0), (0, 0), (0, 1), (1, 1)):
         n = 2 * x + idx + kind * NZ
         away = sib.at[kind * 2 + idx]
-        remote(away, away, s_near.at[0, 0], r_sib.at[kind * 2 + idx], sibling).wait_recv()
+        remote(away, away, s_near.at[0, 0, 0], r_sib.at[kind * 2 + idx], sibling).wait_recv()
         for s in range(2):
             for way in range(2):
-                ref = fin.at[s, kind, idx, way]
                 i = ((s * 2 + kind) * 2 + idx) * 2 + way
-                remote(ref, ref, s_near.at[0, 0], r_fin.at[i], sibling).wait_recv()
+                for half in range(2):
+                    ref = fin.at[s, kind, idx, way, pl.ds(half * SL, SL)]
+                    remote(ref, ref, s_near.at[0, 0, 0], r_fin.at[i, half], sibling).wait_recv()
             own = jnp.where(s == c, near[n, c].astype(F32), sib[kind * 2 + idx].astype(F32))
             total = own + fin[s, kind, idx, 0].astype(F32) + fin[s, kind, idx, 1].astype(F32)
             for i in range(NY):
@@ -487,7 +518,8 @@
         @pl.when(lax.rem(rel, 2) == 1)
         def _():
             for core in range(2):
-                near_copy(n, kind, idx, lax.div(rel, 2), core).wait_send()
+                for half in range(2):
+                    near_copy(n, kind, idx, lax.div(rel, 2), core, half).wait_send()
 
         @pl.when(rel == 0)
         def _():
@@ -513,6 +545,9 @@
         vmem((2 * TOK, HALF), BF16),
         vmem((2 * TOK, HALF), BF16),
         vmem((2 * TOK, HALF), BF16),
+        vmem((HALF, 2 * TOK), BF16),
+        vmem((2 * TOK, HALF), BF16),
+        vmem((HALF, 2 * TOK), BF16),
         vmem((NY, SL, HD), BF16),
         vmem((NY, SL, HD), BF16),
         vmem((NY, SL, HD), F32),
@@ -527,14 +562,15 @@
         vmem((2, 2, 2, 2, rows, TOK), BF16),
         vmem((4, rows, TOK), BF16),
         vmem((2, rows, TOK), F32),
+        vmem((16, 2, SL, TOK), F32),
         vmem((2 * NY, 4, WB, TOK), F32),
         dma((6,)),
         dma((3,)), dma((3,)),
         dma((16,)), dma((16,)), dma((80,)), dma((80,)),
         dma((8,)), dma((8,)), dma((8,)), dma((8,)), dma((8,)), dma((8,)),
         dma((HEADS,)), dma((HEADS,)),
-        dma((16, 2)), dma((16, 2)), dma((16, 2)),
-        dma((16,)), dma((4,)),
+        dma((16, 2)), dma((16, 2)), dma((16, 2, 2)),
+        dma((16, 2)), dma((4,)),
     ]
     operands = (queries, keys, values, head_gain.reshape(1, -1), w_out.T)
     return pl.pallas_call(

time: 60.3 us -> 61.8 us (1.025)
  Pallas kernels: 59.4 us -> 61 us
    pallas_call x1, Pallas kernels: 59.4 us -> 61 us  [per_device(): pl.pallas_call(kernel, out_shape=jax.ShapeDtypeStruct(queries.shape, BF16...]
where the time goes in v4:
time: 61.8 us; the launch traced here: 61.7 us
  Pallas kernels  61 us (99%)
  local copies, waits for them, and re-layouts  0.71 us (1%)
    pallas_call x1, Pallas kernels, per_device(): pl.pallas_call(kernel, out_shape=jax.ShapeDtypeStruct(queries.shape, BF16...  61 us

profile of v4, /device:TPU:1, one launch (start us, length us, event | category | flops | bytes accessed | tf_op | source)
XLA Modules:
  0.0 61.7 jit_solution(13228635274003011876)
XLA Ops:
  0.0 61.0 %shard_map.55 = bf16[128,1024]{1,0:T(8,128)(2,1)S(1)} custom-call(bf16[128,1024]{1,0:T(8,128)(2,1)} %q_ref.1, bf16[128,1024]{1,0:T(8,128)(2,1)} %k_ref.1, bf16[128,1024]{1,0:T(8,128)(2,1)} %v_ref.1, f32[1,1024]{1,0:T(1,128)} %bitcast.3, bf16[32,1024]{1,0:T(8,128)(2,1)} %bitcast.2), custom_call_target="tpu_custom_call" | custom-call | flops 2147483648 | bytes 2097152 | tf_op jit(solution)/shard_map/pallas_call | solution.py:576
  61.0 0.7 %copy.7 = bf16[128,1024]{1,0:T(8,128)(2,1)} copy(bf16[128,1024]{1,0:T(8,128)(2,1)S(1)} %shard_map.55) | data formatting | bytes 524288

commit v5 on v4

--- a/solution.py
+++ b/solution.py
@@ -431,40 +431,60 @@
     line_1()
     queries()
     line_2()
-    ring_recv(1, 1)
+    ring_recv(1, 1, (0,))
+    ring_recv(1, 1, (1,))
     inside(0)
     line_3()
-    ring_recv(1, 2)
+    ring_recv(1, 2, (0,))
+    ring_recv(1, 2, (1,))
     inside(1)
     row_prefix()
-    ring_recv(1, 3)
+    ring_recv(1, 3, (0,))
+    ring_recv(1, 3, (1,))
+    ring_recv(1, 4, (0,))
     inside(2)
-    ring_recv(1, 4)
+    ring_recv(1, 0, (0,))
+    ring_recv(1, 4, (1,))
     inside(3)
-    ring_recv(1, 0)
-    ring_recv(2, 1)
+    ring_recv(1, 0, (1,))
+    ring_recv(2, 1, (0,))
+    ring_recv(2, 1, (1,))
     all_prefix()
-    ring_recv(2, 2)
-    ring_recv(2, 3)
-    ring_recv(2, 4)
-    ring_recv(3, 1)
-    ring_recv(2, 0)
+    ring_recv(2, 2, (0,))
+    ring_recv(2, 3, (0,))
+    ring_recv(2, 2, (1,))
+    ring_recv(2, 3, (1,))
+    ring_recv(2, 4, (0,))
+    ring_recv(2, 4, (1,))
+    ring_recv(3, 1, (0,))
+    ring_recv(3, 1, (1,))
+    ring_recv(2, 0, (0,))
+    ring_recv(2, 0, (1,))
     attend()
-    ring_recv(3, 2)
-    ring_recv(3, 3)
-    ring_recv(3, 4)
-    ring_recv(3, 0)
+    ring_recv(3, 2, (0,))
+    ring_recv(3, 2, (1,))
+    ring_recv(3, 3, (0,))
+    ring_recv(3, 3, (1,))
+    ring_recv(3, 4, (0,))
+    ring_recv(3, 4, (1,))
+    ring_recv(3, 0, (0,))
+    ring_recv(3, 0, (1,))
     swap()
     early_far()
-    ring_recv(4, 1)
-    ring_recv(4, 2)
-    ring_recv(4, 0)
-    ring_recv(4, 3)
-    ring_recv(4, 4)
+    early_near()
+    ring_recv(4, 1, (0,))
+    ring_recv(4, 1, (1,))
+    ring_recv(4, 2, (0,))
+    ring_recv(4, 2, (1,))
+    ring_recv(4, 0, (0,))
+    ring_recv(4, 0, (1,))
+    ring_recv(4, 3, (0,))
+    ring_recv(4, 3, (1,))
+    ring_recv(4, 4, (0,))
+    ring_recv(4, 4, (1,))
     late_far()
-    early_near()
+    early_sum()
     late_near()
-    early_sum()
     late_sum()
     for kind, idx in ((1, 0), (0, 0), (0, 1), (1, 1)):
         n = 2 * x + idx + kind * NZ

time: 61.8 us -> 60.6 us (0.981)
  Pallas kernels: 61 us -> 59.8 us
    pallas_call x1, Pallas kernels: 61 us -> 59.8 us  [per_device(): pl.pallas_call(kernel, out_shape=jax.ShapeDtypeStruct(queries.shape, BF16...]
where the time goes in v5:
time: 60.6 us; the launch traced here: 60.5 us
  Pallas kernels  59.8 us (99%)
  local copies, waits for them, and re-layouts  0.71 us (1%)
    pallas_call x1, Pallas kernels, per_device(): pl.pallas_call(kernel, out_shape=jax.ShapeDtypeStruct(queries.shape, BF16...  59.8 us

profile of v5, /device:TPU:1, one launch (start us, length us, event | category | flops | bytes accessed | tf_op | source)
XLA Modules:
  0.0 60.5 jit_solution(14510076106785793825)
XLA Ops:
  0.0 59.8 %shard_map.55 = bf16[128,1024]{1,0:T(8,128)(2,1)S(1)} custom-call(bf16[128,1024]{1,0:T(8,128)(2,1)} %q_ref.1, bf16[128,1024]{1,0:T(8,128)(2,1)} %k_ref.1, bf16[128,1024]{1,0:T(8,128)(2,1)} %v_ref.1, f32[1,1024]{1,0:T(1,128)} %bitcast.3, bf16[32,1024]{1,0:T(8,128)(2,1)} %bitcast.2), custom_call_target="tpu_custom_call" | custom-call | flops 2147483648 | bytes 2097152 | tf_op jit(solution)/shard_map/pallas_call | solution.py:596
  59.8 0.7 %copy.7 = bf16[128,1024]{1,0:T(8,128)(2,1)} copy(bf16[128,1024]{1,0:T(8,128)(2,1)S(1)} %shard_map.55) | data formatting | bytes 524288
